TPU v7x, 32 devices: a whole 2x2x4 slice. The times are simulated.
32 devices in a mesh: gx: 4 (over z), gy: 4 (over y, x), gz: 2 (over core).
Axes of the slice: x: 2, y: 2, z: 4, core: 2. Of those that a mesh axis runs over, the one named last changes fastest.
Arguments:
- bin_mass: float32 [4, 4, 12, 8, 8, 8, 128], P('gx', 'gy', 'gz'), may hold values from 0.1 to 1
- wind_field: float32 [4, 4, 12, 2, 8, 64], P('gx', 'gy', 'gz'), may hold values from -0.3 to 0.3
- fall_speed: float32 [128], replicated, may hold values from 0.02 to 0.4
- gain_a: float32 [128, 128], replicated, may hold values from -0.5 to 0.5
- gain_b: float32 [128, 128], replicated, may hold values from -0.5 to 0.5
- gain_c: float32 [128, 128], replicated, may hold values from -0.5 to 0.5
- loss_k: float32 [128, 128], replicated, may hold values from -0.5 to 0.5
- old_occupied: int32 [4, 4, 6], P('gx', 'gy'), may hold values from 0 to 1, as said below
- old_neighbours: int32 [4, 4, 6, 4], P('gx', 'gy'), may hold values from -1 to 8, as said below
- old_sends: int32 [4, 4, 4, 3], P('gx', 'gy'), may hold values from -1 to 5, as said below
- old_substeps: int32 [1, 4, 4, 12], P(None, 'gx', 'gy', 'gz'), may hold values from 1 to 4
- move_lists: int32 [4, 4, 3, 2], P('gx', 'gy'), may hold values from -1 to 5, as said below
- new_sources: int32 [4, 4, 6], P('gx', 'gy'), may hold values from -1 to 11, as said below
- new_neighbours: int32 [4, 4, 6, 4], P('gx', 'gy'), may hold values from -1 to 8, as said below
- new_sends: int32 [4, 4, 4, 3], P('gx', 'gy'), may hold values from -1 to 5, as said below
- new_substeps: int32 [1, 4, 4, 12], P(None, 'gx', 'gy', 'gz'), may hold values from 1 to 4
Outputs:
- final_mass: float32 [4, 4, 12, 8, 8, 8, 128], P('gx', 'gy', 'gz')
Inputs may be any that keep to these rules, and one draw needn't show every extreme that they name: `old_occupied`: slots marked 1 hold blocks before the move; some position has all 6 marked. `old_neighbours`: -1 marks the domain's edge or an empty slot; a value under 6 is a slot of the same device; a value 6 + k is entry k of the list that the device next on that side keeps for the opposite side. Lists before and after the move are consistent with each other and with the send lists. `old_sends`: entries are occupied slots of the device, -1 pads; some list holds 3 entries. `move_lists`: entries are occupied old slots, each block sent at most once, -1 pads; routes 0 and 1 each hold 2 entries on some device. `new_sources`: -1 marks an empty slot; a value under 6 is an own old slot that stays; 6 + r * 2 + k is entry k of route r of the sending device; every block has exactly one new slot. `new_neighbours`: as old_neighbours, for the layout after the move. `new_sends`: as old_sends, for the layout after the move.
All inputs are finite; a program needn't handle non-finite values.
Results may differ from a plain program's by a relative error of at most 0.0003.
Values sent between devices are 32-bit elements; how exact they have to be, the bound alone decides.
A program may use at most 64 MiB of HBM per device.

v0:
```python
import functools

import jax
import jax.numpy as jnp
from jax import lax
from jax.experimental import pallas as pl
from jax.experimental.pallas import tpu as pltpu
from jax.sharding import PartitionSpec as P

step_time = 0.25
most_turns = 4
opposite = (1, 0, 3, 2)
MESH = pl.DeviceIdType.MESH


def split(values):
    high = values.astype(jnp.bfloat16)
    low = (values - high.astype(jnp.float32)).astype(jnp.bfloat16)
    return high, low


def kernel(dims, *refs):
    far_mass, far_small, out_ref = refs[0], refs[1:16], refs[16]
    mass_ref, small_refs, (fetched_mass, fetched_small) = refs[17], refs[18:33], refs[33:35]
    wind_ref, fall_ref, gain_a_ref, gain_b_ref, gain_c_ref, loss_k_ref = small_refs[:6]
    occupied_ref, old_nb_ref, old_sends_ref, old_turns_ref, moves_ref = small_refs[6:11]
    sources_ref, new_nb_ref, new_sends_ref, new_turns_ref = small_refs[11:]
    state, done, parcel, arrived, face_x, face_y, send_x, send_y = refs[35:43]
    got_x_old, got_x_new, got_y_old, got_y_new, floor = refs[43:48]
    got_floor_old, got_floor_new, map_one, map_two, place = refs[48:53]
    face_out, face_in, floor_out, floor_in, move_out, move_in = refs[53:]
    slots, bx, by, bz, bins, fcap, mcap, peers = dims
    cells = bx * by
    entries = 3 * mcap
    got_x, got_y = (got_x_old, got_x_new), (got_y_old, got_y_new)
    got_floor = (got_floor_old, got_floor_new)
    here = tuple(lax.axis_index(name) for name in ("gx", "gy", "gz"))

    def at(shift):
        there = tuple(own + step for own, step in zip(here, shift))
        inside = True
        for spot, size in zip(there, peers):
            inside = inside & (spot >= 0) & (spot < size)
        return there, inside

    side_shift = ((-1, 0, 0), (1, 0, 0), (0, -1, 0), (0, 1, 0))
    route_shift = ((-1, 0, 0), (0, 1, 0), (-1, 1, 0))
    around = side_shift + ((0, 0, -1), (0, 0, 1), (-1, 1, 0), (1, -1, 0))

    def fetch_mass(slot):
        return pltpu.make_async_copy(
            far_mass.at[slot], mass_ref.at[slot], fetched_mass.at[slot]
        )

    fetches = [
        pltpu.make_async_copy(far, near, fetched_small.at[i])
        for i, (far, near) in enumerate(zip(far_small, small_refs))
    ]
    for fetch in fetches[6:] + fetches[:1]:
        fetch.start()
    for slot in range(slots):
        fetch_mass(slot).start()
    for fetch in fetches[1:6]:
        fetch.start()

    barrier = pltpu.get_barrier_semaphore()
    for shift in around:
        there, inside = at(shift)

        @pl.when(inside)
        def _():
            pl.semaphore_signal(barrier, inc=1, device_id=there, device_id_type=MESH)

    greeted = jnp.int32(0)
    for shift in around:
        greeted = greeted + at(shift)[1].astype(jnp.int32)
    pl.semaphore_wait(barrier, greeted)

    for fetch in fetches[6:] + fetches[:1]:
        fetch.wait()

    moved = [moves_ref[0, 0, e % mcap, e // mcap] for e in range(entries)]
    count = jnp.int32(0)
    rank = []
    for entry in moved:
        rank.append(count)
        count = count + (entry >= 0).astype(jnp.int32)
    where_to = []
    for slot in range(slots):
        spot = count
        goes = jnp.int32(0)
        for entry, spot_of in zip(moved, rank):
            spot = jnp.where(entry == slot, spot_of, spot)
            goes = jnp.where(entry == slot, 1, goes)
        count = count + (1 - goes)
        where_to.append(spot)
    for slot in range(slots):
        taken = jnp.int32(0)
        for other in range(slots):
            taken = jnp.where(where_to[other] == slot, other, taken)
        place[0, slot] = taken
        place[1, slot] = where_to[slot]
    for e in range(entries):
        place[2, e] = jnp.minimum(rank[e], slots - 1)

    def speeds(wind, component, x):
        return jnp.stack([speed_at(wind, component, x, y) for y in range(by)])

    def speed_at(wind, component, x, y):
        lane = (y * 2 + component) * bx + x
        return jnp.broadcast_to(wind[:, lane : lane + 1], (bz, bins))

    def gather_faces(slot, load_x):
        wind = state[slot, cells]
        for x in range(bx):
            rows = load_x(x)
            state[slot, pl.ds(x * by, by)] = rows
            for y in range(by):
                floor[slot, x, pl.ds(y, 1), :] = rows[y, 0:1, :]
            for y, side in ((by - 1, 0), (0, 1)):
                speed = speed_at(wind, 1, x, y)
                bounded = jnp.maximum(speed, 0.0) if side == 0 else jnp.minimum(speed, 0.0)
                face_y[side, slot, x] = bounded * rows[y]
            if x == bx - 1:
                face_x[0, slot] = jnp.maximum(speeds(wind, 0, x), 0.0) * rows
            if x == 0:
                face_x[1, slot] = jnp.minimum(speeds(wind, 0, x), 0.0) * rows

    def exchange(turn, sends_ref):
        copies = []
        for side in range(4):
            local, out, got = (
                (face_x, send_x, got_x) if side < 2 else (face_y, send_y, got_y)
            )
            back = opposite[side]
            there, inside = at(side_shift[side])

            def pick(k, carry, side=side, local=local, out=out, back=back):
                entry = sends_ref[0, k, 0, side]
                rows = local[back % 2, jnp.clip(entry, 0, slots - 1)]
                out[turn, side % 2, k] = jnp.where(entry >= 0, rows, 0.0)
                return carry

            lax.fori_loop(0, fcap, pick, 0)
            copy = pltpu.make_async_remote_copy(
                src_ref=out.at[turn, side % 2],
                dst_ref=got[turn].at[back % 2],
                send_sem=face_out.at[turn, side],
                recv_sem=face_in.at[turn, back],
                device_id=there,
                device_id_type=MESH,
            )
            pl.when(inside)(copy.start)
            copies.append((copy, inside))
        return copies

    def send_floor(turn):
        there, inside = at((0, 0, -1))
        copy = pltpu.make_async_remote_copy(
            src_ref=floor,
            dst_ref=got_floor[turn],
            send_sem=floor_out.at[turn],
            recv_sem=floor_in.at[turn],
            device_id=there,
            device_id_type=MESH,
        )
        pl.when(inside)(copy.start)
        return copy, inside

    def await_faces(turn, floor_copy):
        copy, _ = floor_copy
        _, above_inside = at((0, 0, 1))
        for side in range(4):
            _, inside = at(side_shift[side])
            got = got_x if side < 2 else got_y
            landing = pltpu.make_async_remote_copy(
                src_ref=got[turn].at[side % 2],
                dst_ref=got[turn].at[side % 2],
                send_sem=face_out.at[turn, side],
                recv_sem=face_in.at[turn, side],
                device_id=at(side_shift[side])[0],
                device_id_type=MESH,
            )
            pl.when(inside)(landing.wait_recv)
        pl.when(above_inside)(copy.wait_recv)

    def await_sent(copies, floor_copy):
        for copy, inside in copies + [floor_copy]:
            pl.when(inside)(copy.wait_send)

    def step(turn, slot, nb_ref, turns_ref, target, spot):
        wind = state[slot, cells]
        ghosts = []
        for side in range(4):
            local, got = (face_x, got_x) if side < 2 else (face_y, got_y)
            code = nb_ref[0, 0, side, slot]
            near = local[side % 2, jnp.clip(code, 0, slots - 1)]
            far = got[turn][side % 2, jnp.clip(code - slots, 0, fcap - 1)]
            ghosts.append(jnp.where(code < 0, 0.0, jnp.where(code < slots, near, far)))
        west, east, south, north = ghosts
        has_above = here[2] + 1 < peers[2]
        fall = fall_ref[...].reshape(1, 1, bins)
        level = lax.broadcasted_iota(jnp.int32, (by, bz, bins), 1)
        rows = state[slot, pl.ds(0, by)]
        speed = speeds(wind, 0, 0)
        behind = west
        for x in range(bx):
            upward = jnp.maximum(speed, 0.0) * rows
            downward = jnp.minimum(speed, 0.0) * rows
            if x + 1 < bx:
                later = state[slot, pl.ds((x + 1) * by, by)]
                later_speed = speeds(wind, 0, x + 1)
                ahead = jnp.minimum(later_speed, 0.0) * later
            else:
                ahead = east
            total_x = (upward + ahead) - (behind + downward)
            speed_y = speeds(wind, 1, x)
            up_y = jnp.maximum(speed_y, 0.0) * rows
            down_y = jnp.minimum(speed_y, 0.0) * rows
            ahead_y = jnp.concatenate([down_y[1:], north[x][None]], axis=0)
            behind_y = jnp.concatenate([south[x][None], up_y[:-1]], axis=0)
            total_y = (up_y + ahead_y) - (behind_y + down_y)
            top = jnp.stack(
                [
                    jnp.broadcast_to(got_floor[turn][slot, x, pl.ds(y, 1), :], (bz, bins))
                    for y in range(by)
                ]
            )
            top = jnp.where(has_above, top, 0.0)
            upper = jnp.where(level == bz - 1, top, pltpu.roll(rows, bz - 1, 1))
            target[spot, pl.ds(x * by, by)] = rows - total_x - total_y - fall * (rows - upper)
            behind = upward
            if x + 1 < bx:
                rows, speed = later, later_speed
        turns = turns_ref[0, 0, 0, slot]
        size = step_time / jnp.maximum(jnp.full((1, bins), turns, jnp.int32), 1).astype(jnp.float32)

        def coagulate(index, carry):
            mass = target[spot, pl.ds(0, cells)].reshape(cells * bz, bins)
            high, low = split(mass)
            first = jnp.dot(
                jnp.concatenate([high, low], axis=1),
                map_one[...],
                preferred_element_type=jnp.float32,
            )
            parts = [first[:, i * bins : (i + 1) * bins] for i in range(6)]
            paired = (parts[0] + parts[3]) * (parts[1] + parts[4])
            lost = mass * (parts[2] + parts[5])
            high, low = split(paired)
            second = jnp.dot(
                jnp.concatenate([high, low], axis=1),
                map_two[...],
                preferred_element_type=jnp.float32,
            )
            gained = second[:, :bins] + second[:, bins:]
            changed = jnp.where(index < turns, mass + size * (gained - lost), mass)
            target[spot, pl.ds(0, cells)] = changed.reshape(cells, bz, bins)
            return carry

        lax.fori_loop(0, most_turns, coagulate, 0)

    def first_faces(slot, carry):
        fetch_mass(slot).wait()
        held = occupied_ref[0, 0, slot] > 0
        columns = wind_ref[0, 0, slot].reshape(2 * bx, by * bz).T
        for y in range(by):
            state[slot, cells, :, pl.ds(y * 2 * bx, 2 * bx)] = columns[y * bz : (y + 1) * bz]
        gather_faces(
            slot, lambda x: jnp.where(held, mass_ref[slot, pl.ds(x * by, by)], 0.0)
        )
        return carry

    lax.fori_loop(0, slots, first_faces, 0)
    copies = exchange(0, old_sends_ref)
    floor_copy = send_floor(0)
    for fetch in fetches[1:6]:
        fetch.wait()
    for i, ref in enumerate((gain_a_ref, gain_b_ref, loss_k_ref)):
        for row in (0, bins):
            for part, values in enumerate(split(ref[...])):
                map_one[pl.ds(row, bins), pl.ds((part * 3 + i) * bins, bins)] = values
    for row in (0, bins):
        for part, values in enumerate(split(gain_c_ref[...])):
            map_two[pl.ds(row, bins), pl.ds(part * bins, bins)] = values
    await_faces(0, floor_copy)

    def move_copy(e):
        route = e // mcap
        west_leg = jnp.where(route == 1, 0, -1)
        north_leg = jnp.where(route == 0, 0, 1)
        there, inside = at((west_leg, north_leg, 0))
        _, incoming = at((-west_leg, -north_leg, 0))
        copy = pltpu.make_async_remote_copy(
            src_ref=parcel.at[e],
            dst_ref=arrived.at[e],
            send_sem=move_out.at[e],
            recv_sem=move_in.at[e],
            device_id=there,
            device_id_type=MESH,
        )
        return copy, inside, incoming

    def post(e, carry):
        copy, inside, _ = move_copy(e)
        parcel[e] = done[place[2, e]]
        pl.when(inside)(copy.start)
        return carry

    def first_step(spot, carry):
        slot = place[0, spot]
        step(0, slot, old_nb_ref, old_turns_ref, done, spot)
        done[spot, cells] = state[slot, cells]
        return carry

    def first_and_post(spot, carry):
        first_step(spot, carry)
        return post(spot, carry)

    shared = min(slots, entries)
    lax.fori_loop(0, shared, first_and_post, 0)
    if slots > shared:
        lax.fori_loop(shared, slots, first_step, 0)
    if entries > shared:
        lax.fori_loop(shared, entries, post, 0)
    await_sent(copies, floor_copy)

    def land(e, carry):
        copy, _, incoming = move_copy(e)
        pl.when(incoming)(copy.wait_recv)
        return carry

    lax.fori_loop(0, entries, land, 0)

    def second_faces(slot, carry):
        code = sources_ref[0, 0, slot]
        own = place[1, jnp.clip(code, 0, slots - 1)]
        came = jnp.clip(code - slots, 0, entries - 1)

        def choose(first, length):
            near = done[own, pl.ds(first, length)]
            far = arrived[came, pl.ds(first, length)]
            return jnp.where(code < 0, 0.0, jnp.where(code < slots, near, far))

        state[slot, cells] = choose(cells, 1)[0]
        gather_faces(slot, lambda x: choose(x * by, by))
        return carry

    lax.fori_loop(0, slots, second_faces, 0)
    copies = exchange(1, new_sends_ref)
    floor_copy = send_floor(1)
    await_faces(1, floor_copy)

    def second_step(slot, carry):
        step(1, slot, new_nb_ref, new_turns_ref, out_ref, slot)
        return carry

    lax.fori_loop(0, slots, second_step, 0)
    await_sent(copies, floor_copy)

    def sent(e, carry):
        copy, inside, _ = move_copy(e)
        pl.when(inside)(copy.wait_send)
        return carry

    lax.fori_loop(0, entries, sent, 0)


def on_device(peers, bin_mass, wind_field, fall_speed, *rest):
    slots, bx, by, bz, bins = bin_mass.shape[2:]
    cells = bx * by
    old_sends, move_lists = rest[6], rest[8]
    fcap, mcap = old_sends.shape[-1], move_lists.shape[-1]
    entries = 3 * mcap
    small = [wind_field, fall_speed.reshape(1, bins), *rest]
    for i in (7, 12):
        small[i] = small[i].transpose(0, 1, 3, 2)
    for i in (8, 13):
        small[i] = small[i].transpose(0, 3, 1, 2)
    small[10] = small[10].transpose(0, 1, 3, 2)
    dims = (slots, bx, by, bz, bins, fcap, mcap, peers)
    vmem = pl.BlockSpec(memory_space=pltpu.VMEM)
    hbm = pl.BlockSpec(memory_space=pltpu.HBM)
    f32 = jnp.float32
    result = pl.pallas_call(
        functools.partial(kernel, dims),
        out_shape=jax.ShapeDtypeStruct((slots, cells, bz, bins), f32),
        in_specs=[hbm] * 16,
        out_specs=vmem,
        scratch_shapes=[
            pltpu.VMEM((slots, cells, bz, bins), f32),
            *[pltpu.VMEM(array.shape, f32) for array in small[:6]],
            *[pltpu.SMEM(array.shape, jnp.int32) for array in small[6:]],
            pltpu.SemaphoreType.DMA((slots,)),
            pltpu.SemaphoreType.DMA((len(small),)),
            pltpu.VMEM((slots, cells + 1, bz, bins), f32),
            pltpu.VMEM((slots, cells + 1, bz, bins), f32),
            pltpu.VMEM((entries, cells + 1, bz, bins), f32),
            pltpu.VMEM((entries, cells + 1, bz, bins), f32),
            pltpu.VMEM((2, slots, by, bz, bins), f32),
            pltpu.VMEM((2, slots, bx, bz, bins), f32),
            pltpu.VMEM((2, 2, fcap, by, bz, bins), f32),
            pltpu.VMEM((2, 2, fcap, bx, bz, bins), f32),
            pltpu.VMEM((2, fcap, by, bz, bins), f32),
            pltpu.VMEM((2, fcap, by, bz, bins), f32),
            pltpu.VMEM((2, fcap, bx, bz, bins), f32),
            pltpu.VMEM((2, fcap, bx, bz, bins), f32),
            pltpu.VMEM((slots, bx, by, bins), f32),
            pltpu.VMEM((slots, bx, by, bins), f32),
            pltpu.VMEM((slots, bx, by, bins), f32),
            pltpu.VMEM((2 * bins, 6 * bins), jnp.bfloat16),
            pltpu.VMEM((2 * bins, 2 * bins), jnp.bfloat16),
            pltpu.SMEM((3, max(slots, entries)), jnp.int32),
            pltpu.SemaphoreType.DMA((2, 4)),
            pltpu.SemaphoreType.DMA((2, 4)),
            pltpu.SemaphoreType.DMA((2,)),
            pltpu.SemaphoreType.DMA((2,)),
            pltpu.SemaphoreType.DMA((entries,)),
            pltpu.SemaphoreType.DMA((entries,)),
        ],
        compiler_params=pltpu.CompilerParams(
            collective_id=0, has_side_effects=True, vmem_limit_bytes=56 * 1024 * 1024
        ),
    )(
        bin_mass.reshape(slots, cells, bz, bins),
        *small,
    )
    return result.reshape(bin_mass.shape)


def solution(mesh):
    peers = tuple(mesh.shape[name] for name in ("gx", "gy", "gz"))
    placed = (
        P("gx", "gy", "gz", None, None, None, None),
        P("gx", "gy", "gz", None, None, None),
        P(),
        P(),
        P(),
        P(),
        P(),
        P("gx", "gy", None),
        P("gx", "gy", None, None),
        P("gx", "gy", None, None),
        P(None, "gx", "gy", "gz"),
        P("gx", "gy", None, None),
        P("gx", "gy", None),
        P("gx", "gy", None, None),
        P("gx", "gy", None, None),
        P(None, "gx", "gy", "gz"),
    )
    return jax.shard_map(
        functools.partial(on_device, peers),
        mesh=mesh,
        in_specs=placed,
        out_specs=P("gx", "gy", "gz", None, None, None, None),
        check_vma=False,
    )
```

profile of v0, /device:TPU:6, one launch (start us, length us, event | category | flops | bytes accessed | tf_op | source)
XLA Modules:
  0.0 67.3 jit_solution(9325734541998429336)
XLA Ops:
  0.0 64.6 %shard_map.154 = f32[6,64,8,128]{3,2,1,0:T(8,128)} custom-call(f32[6,64,8,128]{3,2,1,0:T(8,128)} %bitcast.9, f32[1,1,6,2,8,64]{5,4,3,2,1,0:T(8,128)} %refs_1_.1, f32[1,128]{1,0:T(1,128)} %bitcast.15, f32[128,128]{1,0:T(8,128)} %refs_3_.1, f32[128,128]{1,0:T(8,128)} %refs_4_.1, f32[128,128]{1,0:T(8,128)} %refs_5_.1, f32[128,128]{1,0:T(8,128)} %refs_6_.1, ...), custom_call_target="tpu_custom_call" | custom-call | tf_op jit(solution)/shard_map/pallas_call | solution.py:384
  64.6 2.7 %copy.18 = f32[1,1,6,8,8,8,128]{6,5,4,3,2,1,0:T(8,128)} copy(f32[1,1,6,8,8,8,128]{6,5,4,3,2,1,0:T(8,128)} %bitcast.8) | data formatting | bytes 3145728
where the time goes:
time: 67.4 us; the launch traced here: 67.3 us
  Pallas kernels  64.6 us (96%)
  local copies, waits for them, and re-layouts  2.73 us (4%)
    pallas_call x1, Pallas kernels, on_device(): pl.pallas_call(functools.partial(kernel, dims), out_shape=jax.ShapeDtypeS...  64.6 us
    unnamed x1, local copies, waits for them, and re-layouts  2.73 us

commit v1 on v0

--- a/solution.py
+++ b/solution.py
@@ -17,6 +17,12 @@
     high = values.astype(jnp.bfloat16)
     low = (values - high.astype(jnp.float32)).astype(jnp.bfloat16)
     return high, low
+
+
+def product(rows, map_ref):
+    return jnp.dot(
+        jnp.concatenate(split(rows), axis=1), map_ref[...], preferred_element_type=jnp.float32
+    )
 
 
 def kernel(dims, *refs):
@@ -154,21 +160,20 @@
             copies.append((copy, inside))
         return copies
 
-    def send_floor(turn):
-        there, inside = at((0, 0, -1))
-        copy = pltpu.make_async_remote_copy(
-            src_ref=floor,
-            dst_ref=got_floor[turn],
-            send_sem=floor_out.at[turn],
-            recv_sem=floor_in.at[turn],
-            device_id=there,
+    def floor_copy(turn, slot):
+        return pltpu.make_async_remote_copy(
+            src_ref=floor.at[slot],
+            dst_ref=got_floor[turn].at[slot],
+            send_sem=floor_out.at[turn, slot],
+            recv_sem=floor_in.at[turn, slot],
+            device_id=at((0, 0, -1))[0],
             device_id_type=MESH,
         )
-        pl.when(inside)(copy.start)
-        return copy, inside
-
-    def await_faces(turn, floor_copy):
-        copy, _ = floor_copy
+
+    def send_floor(turn, slot):
+        pl.when(at((0, 0, -1))[1])(floor_copy(turn, slot).start)
+
+    def await_faces(turn):
         _, above_inside = at((0, 0, 1))
         for side in range(4):
             _, inside = at(side_shift[side])
@@ -182,11 +187,20 @@
                 device_id_type=MESH,
             )
             pl.when(inside)(landing.wait_recv)
-        pl.when(above_inside)(copy.wait_recv)
-
-    def await_sent(copies, floor_copy):
-        for copy, inside in copies + [floor_copy]:
+
+        @pl.when(above_inside)
+        def _():
+            for slot in range(slots):
+                floor_copy(turn, slot).wait_recv()
+
+    def await_sent(turn, copies):
+        for copy, inside in copies:
             pl.when(inside)(copy.wait_send)
+
+        @pl.when(at((0, 0, -1))[1])
+        def _():
+            for slot in range(slots):
+                floor_copy(turn, slot).wait_send()
 
     def step(turn, slot, nb_ref, turns_ref, target, spot):
         wind = state[slot, cells]
@@ -235,29 +249,26 @@
         turns = turns_ref[0, 0, 0, slot]
         size = step_time / jnp.maximum(jnp.full((1, bins), turns, jnp.int32), 1).astype(jnp.float32)
 
-        def coagulate(index, carry):
-            mass = target[spot, pl.ds(0, cells)].reshape(cells * bz, bins)
-            high, low = split(mass)
-            first = jnp.dot(
-                jnp.concatenate([high, low], axis=1),
-                map_one[...],
-                preferred_element_type=jnp.float32,
-            )
-            parts = [first[:, i * bins : (i + 1) * bins] for i in range(6)]
-            paired = (parts[0] + parts[3]) * (parts[1] + parts[4])
-            lost = mass * (parts[2] + parts[5])
-            high, low = split(paired)
-            second = jnp.dot(
-                jnp.concatenate([high, low], axis=1),
-                map_two[...],
-                preferred_element_type=jnp.float32,
-            )
-            gained = second[:, :bins] + second[:, bins:]
-            changed = jnp.where(index < turns, mass + size * (gained - lost), mass)
-            target[spot, pl.ds(0, cells)] = changed.reshape(cells, bz, bins)
-            return carry
-
-        lax.fori_loop(0, most_turns, coagulate, 0)
+        half = cells // 2
+        lead = [target[spot, pl.ds(i * half, half)].reshape(half * bz, bins) for i in (0, 1)]
+        for index in range(most_turns):
+            firsts = [product(mass, map_one) for mass in lead]
+            lost, seconds = [], []
+            for mass, first in zip(lead, firsts):
+                parts = [first[:, i * bins : (i + 1) * bins] for i in range(6)]
+                lost.append(mass * (parts[2] + parts[5]))
+                paired = (parts[0] + parts[3]) * (parts[1] + parts[4])
+                seconds.append(product(paired, map_two))
+            lead = [
+                jnp.where(
+                    index < turns,
+                    mass + size * (second[:, :bins] + second[:, bins:] - gone),
+                    mass,
+                )
+                for mass, second, gone in zip(lead, seconds, lost)
+            ]
+        for i in (0, 1):
+            target[spot, pl.ds(i * half, half)] = lead[i].reshape(half, bz, bins)
 
     def first_faces(slot, carry):
         fetch_mass(slot).wait()
@@ -268,11 +279,11 @@
         gather_faces(
             slot, lambda x: jnp.where(held, mass_ref[slot, pl.ds(x * by, by)], 0.0)
         )
+        send_floor(0, slot)
         return carry
 
     lax.fori_loop(0, slots, first_faces, 0)
     copies = exchange(0, old_sends_ref)
-    floor_copy = send_floor(0)
     for fetch in fetches[1:6]:
         fetch.wait()
     for i, ref in enumerate((gain_a_ref, gain_b_ref, loss_k_ref)):
@@ -282,7 +293,7 @@
     for row in (0, bins):
         for part, values in enumerate(split(gain_c_ref[...])):
             map_two[pl.ds(row, bins), pl.ds(part * bins, bins)] = values
-    await_faces(0, floor_copy)
+    await_faces(0)
 
     def move_copy(e):
         route = e // mcap
@@ -322,7 +333,7 @@
         lax.fori_loop(shared, slots, first_step, 0)
     if entries > shared:
         lax.fori_loop(shared, entries, post, 0)
-    await_sent(copies, floor_copy)
+    await_sent(0, copies)
 
     def land(e, carry):
         copy, _, incoming = move_copy(e)
@@ -343,19 +354,19 @@
 
         state[slot, cells] = choose(cells, 1)[0]
         gather_faces(slot, lambda x: choose(x * by, by))
+        send_floor(1, slot)
         return carry
 
     lax.fori_loop(0, slots, second_faces, 0)
     copies = exchange(1, new_sends_ref)
-    floor_copy = send_floor(1)
-    await_faces(1, floor_copy)
+    await_faces(1)
 
     def second_step(slot, carry):
         step(1, slot, new_nb_ref, new_turns_ref, out_ref, slot)
         return carry
 
     lax.fori_loop(0, slots, second_step, 0)
-    await_sent(copies, floor_copy)
+    await_sent(1, copies)
 
     def sent(e, carry):
         copy, inside, _ = move_copy(e)
@@ -412,8 +423,8 @@
             pltpu.SMEM((3, max(slots, entries)), jnp.int32),
             pltpu.SemaphoreType.DMA((2, 4)),
             pltpu.SemaphoreType.DMA((2, 4)),
-            pltpu.SemaphoreType.DMA((2,)),
-            pltpu.SemaphoreType.DMA((2,)),
+            pltpu.SemaphoreType.DMA((2, slots)),
+            pltpu.SemaphoreType.DMA((2, slots)),
             pltpu.SemaphoreType.DMA((entries,)),
             pltpu.SemaphoreType.DMA((entries,)),
         ],

time: 67.4 us -> 59.2 us (0.88)
  Pallas kernels: 64.6 us -> 56.3 us
    pallas_call x1, Pallas kernels: 64.6 us -> 56.3 us  [on_device(): pl.pallas_call(functools.partial(kernel, dims), out_shape=jax.ShapeDtypeS...]
where the time goes in v1:
time: 59.2 us; the launch traced here: 59 us
  Pallas kernels  56.3 us (95%)
  local copies, waits for them, and re-layouts  2.73 us (5%)
    pallas_call x1, Pallas kernels, on_device(): pl.pallas_call(functools.partial(kernel, dims), out_shape=jax.ShapeDtypeS...  56.3 us
    unnamed x1, local copies, waits for them, and re-layouts  2.73 us

profile of v1, /device:TPU:6, one launch (start us, length us, event | category | flops | bytes accessed | tf_op | source)
XLA Modules:
  0.0 59.0 jit_solution(7784476959674196984)
XLA Ops:
  0.0 56.3 %shard_map.154 = f32[6,64,8,128]{3,2,1,0:T(8,128)} custom-call(f32[6,64,8,128]{3,2,1,0:T(8,128)} %bitcast.9, f32[1,1,6,2,8,64]{5,4,3,2,1,0:T(8,128)} %refs_1_.1, f32[1,128]{1,0:T(1,128)} %bitcast.15, f32[128,128]{1,0:T(8,128)} %refs_3_.1, f32[128,128]{1,0:T(8,128)} %refs_4_.1, f32[128,128]{1,0:T(8,128)} %refs_5_.1, f32[128,128]{1,0:T(8,128)} %refs_6_.1, ...), custom_call_target="tpu_custom_call" | custom-call | tf_op jit(solution)/shard_map/pallas_call | solution.py:395
  56.3 2.7 %copy.18 = f32[1,1,6,8,8,8,128]{6,5,4,3,2,1,0:T(8,128)} copy(f32[1,1,6,8,8,8,128]{6,5,4,3,2,1,0:T(8,128)} %bitcast.8) | data formatting | bytes 3145728

commit v2 on v1

--- a/solution.py
+++ b/solution.py
@@ -34,7 +34,7 @@
     state, done, parcel, arrived, face_x, face_y, send_x, send_y = refs[35:43]
     got_x_old, got_x_new, got_y_old, got_y_new, floor = refs[43:48]
     got_floor_old, got_floor_new, map_one, map_two, place = refs[48:53]
-    face_out, face_in, floor_out, floor_in, move_out, move_in = refs[53:]
+    face_out, face_in, floor_out, floor_in, move_out, move_in, final, delivered = refs[53:]
     slots, bx, by, bz, bins, fcap, mcap, peers = dims
     cells = bx * by
     entries = 3 * mcap
@@ -132,6 +132,10 @@
             if x == 0:
                 face_x[1, slot] = jnp.minimum(speeds(wind, 0, x), 0.0) * rows
 
+    def kept_at(turn, slot):
+        held = jnp.clip(slot, 0, slots - 1)
+        return place[1, held] if turn == 0 else held
+
     def exchange(turn, sends_ref):
         copies = []
         for side in range(4):
@@ -143,7 +147,7 @@
 
             def pick(k, carry, side=side, local=local, out=out, back=back):
                 entry = sends_ref[0, k, 0, side]
-                rows = local[back % 2, jnp.clip(entry, 0, slots - 1)]
+                rows = local[back % 2, kept_at(turn, entry)]
                 out[turn, side % 2, k] = jnp.where(entry >= 0, rows, 0.0)
                 return carry
 
@@ -174,7 +178,6 @@
         pl.when(at((0, 0, -1))[1])(floor_copy(turn, slot).start)
 
     def await_faces(turn):
-        _, above_inside = at((0, 0, 1))
         for side in range(4):
             _, inside = at(side_shift[side])
             got = got_x if side < 2 else got_y
@@ -188,11 +191,6 @@
             )
             pl.when(inside)(landing.wait_recv)
 
-        @pl.when(above_inside)
-        def _():
-            for slot in range(slots):
-                floor_copy(turn, slot).wait_recv()
-
     def await_sent(turn, copies):
         for copy, inside in copies:
             pl.when(inside)(copy.wait_send)
@@ -203,26 +201,27 @@
                 floor_copy(turn, slot).wait_send()
 
     def step(turn, slot, nb_ref, turns_ref, target, spot):
-        wind = state[slot, cells]
+        wind = state[spot, cells]
+        has_above = here[2] + 1 < peers[2]
+        pl.when(has_above)(floor_copy(turn, spot).wait_recv)
         ghosts = []
         for side in range(4):
             local, got = (face_x, got_x) if side < 2 else (face_y, got_y)
             code = nb_ref[0, 0, side, slot]
-            near = local[side % 2, jnp.clip(code, 0, slots - 1)]
+            near = local[side % 2, kept_at(turn, code)]
             far = got[turn][side % 2, jnp.clip(code - slots, 0, fcap - 1)]
             ghosts.append(jnp.where(code < 0, 0.0, jnp.where(code < slots, near, far)))
         west, east, south, north = ghosts
-        has_above = here[2] + 1 < peers[2]
         fall = fall_ref[...].reshape(1, 1, bins)
         level = lax.broadcasted_iota(jnp.int32, (by, bz, bins), 1)
-        rows = state[slot, pl.ds(0, by)]
+        rows = state[spot, pl.ds(0, by)]
         speed = speeds(wind, 0, 0)
         behind = west
         for x in range(bx):
             upward = jnp.maximum(speed, 0.0) * rows
             downward = jnp.minimum(speed, 0.0) * rows
             if x + 1 < bx:
-                later = state[slot, pl.ds((x + 1) * by, by)]
+                later = state[spot, pl.ds((x + 1) * by, by)]
                 later_speed = speeds(wind, 0, x + 1)
                 ahead = jnp.minimum(later_speed, 0.0) * later
             else:
@@ -236,7 +235,7 @@
             total_y = (up_y + ahead_y) - (behind_y + down_y)
             top = jnp.stack(
                 [
-                    jnp.broadcast_to(got_floor[turn][slot, x, pl.ds(y, 1), :], (bz, bins))
+                    jnp.broadcast_to(got_floor[turn][spot, x, pl.ds(y, 1), :], (bz, bins))
                     for y in range(by)
                 ]
             )
@@ -270,18 +269,20 @@
         for i in (0, 1):
             target[spot, pl.ds(i * half, half)] = lead[i].reshape(half, bz, bins)
 
-    def first_faces(slot, carry):
-        fetch_mass(slot).wait()
+    def first_faces(spot, carry):
+        slot = place[0, spot]
         held = occupied_ref[0, 0, slot] > 0
         columns = wind_ref[0, 0, slot].reshape(2 * bx, by * bz).T
         for y in range(by):
-            state[slot, cells, :, pl.ds(y * 2 * bx, 2 * bx)] = columns[y * bz : (y + 1) * bz]
+            state[spot, cells, :, pl.ds(y * 2 * bx, 2 * bx)] = columns[y * bz : (y + 1) * bz]
         gather_faces(
-            slot, lambda x: jnp.where(held, mass_ref[slot, pl.ds(x * by, by)], 0.0)
+            spot, lambda x: jnp.where(held, mass_ref[slot, pl.ds(x * by, by)], 0.0)
         )
-        send_floor(0, slot)
-        return carry
-
+        send_floor(0, spot)
+        return carry
+
+    for slot in range(slots):
+        fetch_mass(slot).wait()
     lax.fori_loop(0, slots, first_faces, 0)
     copies = exchange(0, old_sends_ref)
     for fetch in fetches[1:6]:
@@ -320,7 +321,7 @@
     def first_step(spot, carry):
         slot = place[0, spot]
         step(0, slot, old_nb_ref, old_turns_ref, done, spot)
-        done[spot, cells] = state[slot, cells]
+        done[spot, cells] = state[spot, cells]
         return carry
 
     def first_and_post(spot, carry):
@@ -362,10 +363,16 @@
     await_faces(1)
 
     def second_step(slot, carry):
-        step(1, slot, new_nb_ref, new_turns_ref, out_ref, slot)
-        return carry
+        step(1, slot, new_nb_ref, new_turns_ref, final, slot)
+        deliver(slot).start()
+        return carry
+
+    def deliver(slot):
+        return pltpu.make_async_copy(final.at[slot], out_ref.at[slot], delivered.at[slot])
 
     lax.fori_loop(0, slots, second_step, 0)
+    for slot in range(slots):
+        deliver(slot).wait()
     await_sent(1, copies)
 
     def sent(e, carry):
@@ -389,14 +396,13 @@
         small[i] = small[i].transpose(0, 3, 1, 2)
     small[10] = small[10].transpose(0, 1, 3, 2)
     dims = (slots, bx, by, bz, bins, fcap, mcap, peers)
-    vmem = pl.BlockSpec(memory_space=pltpu.VMEM)
     hbm = pl.BlockSpec(memory_space=pltpu.HBM)
     f32 = jnp.float32
     result = pl.pallas_call(
         functools.partial(kernel, dims),
         out_shape=jax.ShapeDtypeStruct((slots, cells, bz, bins), f32),
         in_specs=[hbm] * 16,
-        out_specs=vmem,
+        out_specs=hbm,
         scratch_shapes=[
             pltpu.VMEM((slots, cells, bz, bins), f32),
             *[pltpu.VMEM(array.shape, f32) for array in small[:6]],
@@ -427,6 +433,8 @@
             pltpu.SemaphoreType.DMA((2, slots)),
             pltpu.SemaphoreType.DMA((entries,)),
             pltpu.SemaphoreType.DMA((entries,)),
+            pltpu.VMEM((slots, cells, bz, bins), f32),
+            pltpu.SemaphoreType.DMA((slots,)),
         ],
         compiler_params=pltpu.CompilerParams(
             collective_id=0, has_side_effects=True, vmem_limit_bytes=56 * 1024 * 1024

time: 59.2 us -> 58.7 us (level)
  no operation moved by 1% of the time
where the time goes in v2:
time: 58.7 us; the launch traced here: 58.6 us
  Pallas kernels  55.8 us (95%)
  local copies, waits for them, and re-layouts  2.73 us (5%)
    pallas_call x1, Pallas kernels, on_device(): pl.pallas_call(functools.partial(kernel, dims), out_shape=jax.ShapeDtypeS...  55.8 us
    unnamed x1, local copies, waits for them, and re-layouts  2.73 us

profile of v2, /device:TPU:6, one launch (start us, length us, event | category | flops | bytes accessed | tf_op | source)
XLA Modules:
  0.0 58.6 jit_solution(17509563155824889725)
XLA Ops:
  0.0 55.8 %shard_map.154 = f32[6,64,8,128]{3,2,1,0:T(8,128)} custom-call(f32[6,64,8,128]{3,2,1,0:T(8,128)} %bitcast.9, f32[1,1,6,2,8,64]{5,4,3,2,1,0:T(8,128)} %refs_1_.1, f32[1,128]{1,0:T(1,128)} %bitcast.15, f32[128,128]{1,0:T(8,128)} %refs_3_.1, f32[128,128]{1,0:T(8,128)} %refs_4_.1, f32[128,128]{1,0:T(8,128)} %refs_5_.1, f32[128,128]{1,0:T(8,128)} %refs_6_.1, ...), custom_call_target="tpu_custom_call" | custom-call | tf_op jit(solution)/shard_map/pallas_call | solution.py:401
  55.8 2.7 %copy.18 = f32[1,1,6,8,8,8,128]{6,5,4,3,2,1,0:T(8,128)} copy(f32[1,1,6,8,8,8,128]{6,5,4,3,2,1,0:T(8,128)} %bitcast.8) | data formatting | bytes 3145728

commit v3 on v1

--- a/solution.py
+++ b/solution.py
@@ -34,7 +34,7 @@
     state, done, parcel, arrived, face_x, face_y, send_x, send_y = refs[35:43]
     got_x_old, got_x_new, got_y_old, got_y_new, floor = refs[43:48]
     got_floor_old, got_floor_new, map_one, map_two, place = refs[48:53]
-    face_out, face_in, floor_out, floor_in, move_out, move_in = refs[53:]
+    face_out, face_in, floor_out, floor_in, move_out, move_in, final, delivered = refs[53:]
     slots, bx, by, bz, bins, fcap, mcap, peers = dims
     cells = bx * by
     entries = 3 * mcap
@@ -85,7 +85,15 @@
     for fetch in fetches[6:] + fetches[:1]:
         fetch.wait()
 
-    moved = [moves_ref[0, 0, e % mcap, e // mcap] for e in range(entries)]
+    def entry_at(turn):
+        route = turn // mcap
+        turned = jnp.where(route < 2, 1 - route, route)
+        return jnp.where(here[2] % 2 == 0, route, turned), turn % mcap
+
+    moved = []
+    for turn in range(entries):
+        route, k = entry_at(turn)
+        moved.append(moves_ref[0, 0, k, route])
     count = jnp.int32(0)
     rank = []
     for entry in moved:
@@ -311,9 +319,11 @@
         )
         return copy, inside, incoming
 
-    def post(e, carry):
+    def post(turn, carry):
+        route, k = entry_at(turn)
+        e = route * mcap + k
         copy, inside, _ = move_copy(e)
-        parcel[e] = done[place[2, e]]
+        parcel[e] = done[place[2, turn]]
         pl.when(inside)(copy.start)
         return carry
 
@@ -362,10 +372,16 @@
     await_faces(1)
 
     def second_step(slot, carry):
-        step(1, slot, new_nb_ref, new_turns_ref, out_ref, slot)
-        return carry
+        step(1, slot, new_nb_ref, new_turns_ref, final, slot)
+        deliver(slot).start()
+        return carry
+
+    def deliver(slot):
+        return pltpu.make_async_copy(final.at[slot], out_ref.at[slot], delivered.at[slot])
 
     lax.fori_loop(0, slots, second_step, 0)
+    for slot in range(slots):
+        deliver(slot).wait()
     await_sent(1, copies)
 
     def sent(e, carry):
@@ -389,14 +405,13 @@
         small[i] = small[i].transpose(0, 3, 1, 2)
     small[10] = small[10].transpose(0, 1, 3, 2)
     dims = (slots, bx, by, bz, bins, fcap, mcap, peers)
-    vmem = pl.BlockSpec(memory_space=pltpu.VMEM)
     hbm = pl.BlockSpec(memory_space=pltpu.HBM)
     f32 = jnp.float32
     result = pl.pallas_call(
         functools.partial(kernel, dims),
         out_shape=jax.ShapeDtypeStruct((slots, cells, bz, bins), f32),
         in_specs=[hbm] * 16,
-        out_specs=vmem,
+        out_specs=hbm,
         scratch_shapes=[
             pltpu.VMEM((slots, cells, bz, bins), f32),
             *[pltpu.VMEM(array.shape, f32) for array in small[:6]],
@@ -427,6 +442,8 @@
             pltpu.SemaphoreType.DMA((2, slots)),
             pltpu.SemaphoreType.DMA((entries,)),
             pltpu.SemaphoreType.DMA((entries,)),
+            pltpu.VMEM((slots, cells, bz, bins), f32),
+            pltpu.SemaphoreType.DMA((slots,)),
         ],
         compiler_params=pltpu.CompilerParams(
             collective_id=0, has_side_effects=True, vmem_limit_bytes=56 * 1024 * 1024

time: 59.2 us -> 58.4 us (0.986)
  Pallas kernels: 56.3 us -> 55.6 us
    pallas_call x1, Pallas kernels: 56.3 us -> 55.6 us  [on_device(): pl.pallas_call(functools.partial(kernel, dims), out_shape=jax.ShapeDtypeS...]
where the time goes in v3:
time: 58.4 us; the launch traced here: 58.3 us
  Pallas kernels  55.6 us (95%)
  local copies, waits for them, and re-layouts  2.73 us (5%)
    pallas_call x1, Pallas kernels, on_device(): pl.pallas_call(functools.partial(kernel, dims), out_shape=jax.ShapeDtypeS...  55.6 us
    unnamed x1, local copies, waits for them, and re-layouts  2.73 us

profile of v3, /device:TPU:6, one launch (start us, length us, event | category | flops | bytes accessed | tf_op | source)
XLA Modules:
  0.0 58.3 jit_solution(7644718449183133947)
XLA Ops:
  0.0 55.6 %shard_map.154 = f32[6,64,8,128]{3,2,1,0:T(8,128)} custom-call(f32[6,64,8,128]{3,2,1,0:T(8,128)} %bitcast.9, f32[1,1,6,2,8,64]{5,4,3,2,1,0:T(8,128)} %refs_1_.1, f32[1,128]{1,0:T(1,128)} %bitcast.15, f32[128,128]{1,0:T(8,128)} %refs_3_.1, f32[128,128]{1,0:T(8,128)} %refs_4_.1, f32[128,128]{1,0:T(8,128)} %refs_5_.1, f32[128,128]{1,0:T(8,128)} %refs_6_.1, ...), custom_call_target="tpu_custom_call" | custom-call | tf_op jit(solution)/shard_map/pallas_call | solution.py:410
  55.6 2.7 %copy.18 = f32[1,1,6,8,8,8,128]{6,5,4,3,2,1,0:T(8,128)} copy(f32[1,1,6,8,8,8,128]{6,5,4,3,2,1,0:T(8,128)} %bitcast.8) | data formatting | bytes 3145728

commit v4 on v3

--- a/solution.py
+++ b/solution.py
@@ -257,8 +257,12 @@
         turns = turns_ref[0, 0, 0, slot]
         size = step_time / jnp.maximum(jnp.full((1, bins), turns, jnp.int32), 1).astype(jnp.float32)
 
-        half = cells // 2
-        lead = [target[spot, pl.ds(i * half, half)].reshape(half * bz, bins) for i in (0, 1)]
+        pieces = 4 if cells % 4 == 0 else 1
+        part_cells = cells // pieces
+        lead = [
+            target[spot, pl.ds(i * part_cells, part_cells)].reshape(part_cells * bz, bins)
+            for i in range(pieces)
+        ]
         for index in range(most_turns):
             firsts = [product(mass, map_one) for mass in lead]
             lost, seconds = [], []
@@ -275,8 +279,10 @@
                 )
                 for mass, second, gone in zip(lead, seconds, lost)
             ]
-        for i in (0, 1):
-            target[spot, pl.ds(i * half, half)] = lead[i].reshape(half, bz, bins)
+        for i in range(pieces):
+            target[spot, pl.ds(i * part_cells, part_cells)] = lead[i].reshape(
+                part_cells, bz, bins
+            )
 
     def first_faces(slot, carry):
         fetch_mass(slot).wait()

time: 58.4 us -> 58.4 us (level)
  no operation moved by 1% of the time
where the time goes in v4:
time: 58.4 us; the launch traced here: 58.2 us
  Pallas kernels  55.5 us (95%)
  local copies, waits for them, and re-layouts  2.73 us (5%)
    pallas_call x1, Pallas kernels, on_device(): pl.pallas_call(functools.partial(kernel, dims), out_shape=jax.ShapeDtypeS...  55.5 us
    unnamed x1, local copies, waits for them, and re-layouts  2.73 us

profile of v4, /device:TPU:6, one launch (start us, length us, event | category | flops | bytes accessed | tf_op | source)
XLA Modules:
  0.0 58.2 jit_solution(4036678708788961004)
XLA Ops:
  0.0 55.5 %shard_map.154 = f32[6,64,8,128]{3,2,1,0:T(8,128)} custom-call(f32[6,64,8,128]{3,2,1,0:T(8,128)} %bitcast.9, f32[1,1,6,2,8,64]{5,4,3,2,1,0:T(8,128)} %refs_1_.1, f32[1,128]{1,0:T(1,128)} %bitcast.15, f32[128,128]{1,0:T(8,128)} %refs_3_.1, f32[128,128]{1,0:T(8,128)} %refs_4_.1, f32[128,128]{1,0:T(8,128)} %refs_5_.1, f32[128,128]{1,0:T(8,128)} %refs_6_.1, ...), custom_call_target="tpu_custom_call" | custom-call | tf_op jit(solution)/shard_map/pallas_call | solution.py:416
  55.5 2.7 %copy.18 = f32[1,1,6,8,8,8,128]{6,5,4,3,2,1,0:T(8,128)} copy(f32[1,1,6,8,8,8,128]{6,5,4,3,2,1,0:T(8,128)} %bitcast.8) | data formatting | bytes 3145728
